TPU v7x, 128 devices: a whole 4x4x4 slice. The times are simulated.
128 devices in a mesh: row: 16 (over z_lo, y, core), col: 8 (over x, z_hi).
Axes of the slice: x: 4, y: 4, z: 4 (z_hi: 2, z_lo: 2; z = z_hi * 2 + z_lo), core: 2. Of those that a mesh axis runs over, the one named last changes fastest.
Arguments:
- coeffs: float32 [16, 8, 8, 8, 64, 512], P('row', 'col'), may hold values from -6 to 6
- row_weights: float32 [3, 16, 8, 8, 8, 64, 128], P(None, 'row', 'col'), may hold values from -0.5 to 0.5
- col_weights: float32 [3, 16, 8, 8, 8, 64, 128], P(None, 'row', 'col'), may hold values from -0.5 to 0.5
Outputs:
- result: float32 [16, 8, 8, 8, 64, 512], P('row', 'col')
All inputs are finite; a program needn't handle non-finite values.
Results may differ from a plain program's by a relative error of at most 0.00013.
Values sent between devices are 32-bit elements; how exact they have to be, the bound alone decides.
A program may use at most 128 MiB of HBM per device.

v0:
```python
import jax
import jax.numpy as jnp
from jax import lax
from jax.sharding import PartitionSpec as P


def swapped(value, axis, distance):
    mask = 2**distance
    pairs = [(source, source ^ mask) for source in range(lax.axis_size(axis))]
    return lax.ppermute(value, axis, pairs)


def flip_axis(values, axis, stride):
    shape = values.shape
    split = shape[:axis] + (shape[axis] // (2 * stride), 2, stride) + shape[axis + 1 :]
    return jnp.flip(values.reshape(split), axis=axis + 1).reshape(shape)


def mix_level(weights, state, partner):
    joined = jnp.concatenate([state, partner], axis=-2)
    return jnp.einsum("...xy,...ys->...xs", weights, joined, precision=lax.Precision.HIGHEST)


def per_device(coeffs, row_weights, col_weights):
    groups = coeffs.shape[2]
    tail = coeffs.shape[3]
    rank = coeffs.shape[4]
    width = coeffs.shape[5]
    n_row = lax.axis_size("row")
    row_levels = row_weights.shape[0]
    col_levels = col_weights.shape[0]
    blocks = groups * tail
    state = coeffs.reshape(blocks, rank, width)
    for level in range(row_levels):
        stride = n_row >> level + 1
        partner = swapped(state, "row", stride.bit_length() - 1)
        weights = row_weights[level].reshape(blocks, rank, 2 * rank)
        state = mix_level(weights, state, partner)
    arranged = lax.all_to_all(
        state.reshape(groups, 1, tail, rank, width), "col", split_axis=0, concat_axis=1, tiled=True
    )
    state = arranged.reshape(blocks, rank, width)
    for level in range(col_levels):
        stride = blocks >> level + 1
        weights = col_weights[level].reshape(blocks, rank, 2 * rank)
        state = mix_level(weights, state, flip_axis(state, 0, stride))
    return state.reshape(coeffs.shape)


def solution(mesh):
    return jax.shard_map(
        per_device,
        mesh=mesh,
        in_specs=(
            P("row", "col", None, None, None, None),
            P(None, "row", "col", None, None, None, None),
            P(None, "row", "col", None, None, None, None),
        ),
        out_specs=P("row", "col", None, None, None, None),
        check_vma=False,
    )
```

profile of v0, /device:TPU:0, one launch (start us, length us, event | category | flops | bytes accessed | tf_op | source)
XLA Modules:
  0.0 791.3 jit_solution(5405390558294266671)
XLA Ops:
  0.0 2.0 collective-permute-start
  2.0 5.7 fusion.36
  7.7 174.9 %collective-permute-done = f32[64,64,512]{2,1,0:T(8,128)S(1)} collective-permute-done((f32[64,64,512]{2,1,0:T(8,128)}, f32[64,64,512]{2,1,0:T(8,128)S(1)}, u32[]{:S(2)}, u32[]{:S(2)}) %collective-permute-start) | collective-permute-done | bytes 8388640 | tf_op jit(solution)/shard_map/ppermute | solution.py:10
  182.7 0.0 copy-start.1
  182.7 3.4 copy-done.1
  186.1 13.6 %fusion.27 = f32[64,64,512]{2,1,0:T(8,128)S(1)} fusion(f32[64,64,128]{2,1,0:T(8,128)} %bitcast.51, f32[64,64,512]{2,1,0:T(8,128)} %copy-done.1, f32[64,64,512]{2,1,0:T(8,128)} %bitcast.45), kind=kOutput, calls=%fused_computation.25 | convolution fusion | flops 3225419776 | bytes 27262976 | tf_op jit(solution)/shard_map/...xy,...ys->...xs/dot_general | solution.py:21
  199.7 0.0 copy-start
  199.7 3.3 collective-permute-start.1
  203.0 179.9 %collective-permute-done.1 = f32[64,64,512]{2,1,0:T(8,128)S(1)} collective-permute-done((f32[64,64,512]{2,1,0:T(8,128)S(1)}, f32[64,64,512]{2,1,0:T(8,128)S(1)}, u32[]{:S(2)}, u32[]{:S(2)}) %collective-permute-start.1) | collective-permute-done | bytes 8388640 | tf_op jit(solution)/shard_map/ppermute | solution.py:10
  382.9 0.0 copy-start.3
  382.9 0.0 copy-done
  382.9 3.4 copy-done.3
  386.3 13.6 %fusion.24 = f32[64,64,512]{2,1,0:T(8,128)S(1)} fusion(f32[64,64,128]{2,1,0:T(8,128)} %bitcast.48, f32[64,64,512]{2,1,0:T(8,128)} %copy-done.3, f32[64,64,512]{2,1,0:T(8,128)} %copy-done), kind=kOutput, calls=%fused_computation.24 | convolution fusion | flops 3225419776 | bytes 27262976 | tf_op jit(solution)/shard_map/...xy,...ys->...xs/dot_general | solution.py:21
  399.9 1.7 collective-permute-start.2
  401.6 179.2 %collective-permute-done.2 = f32[64,64,512]{2,1,0:T(8,128)S(1)} collective-permute-done((f32[64,64,512]{2,1,0:T(8,128)S(1)}, f32[64,64,512]{2,1,0:T(8,128)S(1)}, u32[]{:S(2)}, u32[]{:S(2)}) %collective-permute-start.2) | collective-permute-done | bytes 8388640 | tf_op jit(solution)/shard_map/ppermute | solution.py:10
  580.9 0.0 copy-start.2
  580.9 3.4 copy-done.2
  584.2 14.1 %fusion.8 = f32[64,512,64]{1,2,0:T(8,128)} fusion(f32[64,64,128]{2,1,0:T(8,128)} %bitcast.46, f32[64,64,512]{2,1,0:T(8,128)} %copy-done.2, f32[64,64,512]{2,1,0:T(8,128)S(1)} %fusion.24), kind=kOutput, calls=%fused_computation.8 | convolution fusion | flops 3225419776 | bytes 27262976 | tf_op jit(solution)/shard_map/...xy,...ys->...xs/dot_general | solution.py:21
  598.3 6.9 all-to-all-start
  605.2 5.8 fusion.37
  610.9 107.3 %all-to-all-done = f32[8,1,8,64,512]{4,3,2,1,0:T(8,128)} async-done(((f32[8,1,8,64,512]{4,3,2,1,0:T(8,128)}), f32[8,1,8,64,512]{4,3,2,1,0:T(8,128)}, u32[]{:S(2)}, u32[]{:S(2)}) %all-to-all-start) | async-done | bytes 8388640 | tf_op jit(solution)/shard_map/all_to_all | solution.py:39
  718.2 8.6 %rev.12 = f32[1,2,32,64,512]{4,3,2,1,0:T(8,128)} reverse(f32[1,2,32,64,512]{4,3,2,1,0:T(8,128)} %bitcast.10), dimensions={1} | reverse | bytes 16777216 | tf_op jit(solution)/shard_map/jit(_flip)/rev | solution.py:16
  726.8 16.1 %fusion.12 = f32[64,512,64]{1,2,0:T(8,128)} fusion(f32[64,64,128]{2,1,0:T(8,128)} %bitcast.50, f32[64,64,512]{2,1,0:T(8,128)} %bitcast.42, f32[64,64,512]{2,1,0:T(8,128)} %bitcast.9), kind=kOutput, calls=%fused_computation.12 | convolution fusion | flops 3225419776 | bytes 27262976 | tf_op jit(solution)/shard_map/...xy,...ys->...xs/dot_general | solution.py:21
  743.0 8.6 %rev.13 = f32[2,2,16,64,512]{4,3,2,1,0:T(8,128)} reverse(f32[2,2,16,64,512]{4,3,2,1,0:T(8,128)} %bitcast.38), dimensions={1} | reverse | bytes 16777216 | tf_op jit(solution)/shard_map/jit(_flip)/rev | solution.py:16
  751.6 16.2 %fusion.16 = f32[64,512,64]{1,2,0:T(8,128)} fusion(f32[64,64,128]{2,1,0:T(8,128)} %bitcast.49, f32[64,64,512]{2,1,0:T(8,128)} %bitcast.43, f32[64,64,512]{2,1,0:T(8,128)} %bitcast.39), kind=kOutput, calls=%fused_computation.16 | convolution fusion | flops 3225419776 | bytes 27262976 | tf_op jit(solution)/shard_map/...xy,...ys->...xs/dot_general | solution.py:21
  767.7 8.4 %rev.14 = f32[4,2,8,64,512]{4,3,2,1,0:T(8,128)} reverse(f32[4,2,8,64,512]{4,3,2,1,0:T(8,128)} %bitcast.36), dimensions={1} | reverse | bytes 16777216 | tf_op jit(solution)/shard_map/jit(_flip)/rev | solution.py:16
  776.2 15.1 %fusion.20 = f32[64,512,64]{1,2,0:T(8,128)} fusion(f32[64,64,128]{2,1,0:T(8,128)S(1)} %bitcast.47, f32[64,64,512]{2,1,0:T(8,128)} %bitcast.41, f32[64,64,512]{2,1,0:T(8,128)} %bitcast.37), kind=kOutput, calls=%fused_computation.20 | convolution fusion | flops 3225419776 | bytes 27262976 | tf_op jit(solution)/shard_map/...xy,...ys->...xs/dot_general | solution.py:21
Async XLA Ops:
  0.0 182.7 %collective-permute-start = (f32[64,64,512]{2,1,0:T(8,128)}, f32[64,64,512]{2,1,0:T(8,128)S(1)}, u32[]{:S(2)}, u32[]{:S(2)}) collective-permute-start(f32[64,64,512]{2,1,0:T(8,128)} %bitcast.44), channel_id=1, source_target_pairs={{0,64},{8,72},{16,80},{24,88},{32,96},{40,104},{48,112},{56,120},{... | collective-permute-start | bytes 25165832 | tf_op jit(solution)/shard_map/ppermute | solution.py:10
  182.7 3.4 copy-start.1
  199.7 183.2 %copy-start = (f32[64,64,512]{2,1,0:T(8,128)}, f32[64,64,512]{2,1,0:T(8,128)S(1)}, u32[]{:S(2)}) copy-start(f32[64,64,512]{2,1,0:T(8,128)S(1)} %fusion.27) | copy-start | bytes 25165828
  199.7 183.2 %collective-permute-start.1 = (f32[64,64,512]{2,1,0:T(8,128)S(1)}, f32[64,64,512]{2,1,0:T(8,128)S(1)}, u32[]{:S(2)}, u32[]{:S(2)}) collective-permute-start(f32[64,64,512]{2,1,0:T(8,128)S(1)} %fusion.27), channel_id=1, source_target_pairs={{0,32},{8,40},{16,48},{24,56},{32,0},{40,8},{48,16},{56,24},{64,96... | collective-permute-start | bytes 25165832 | tf_op jit(solution)/shard_map/ppermute | solution.py:10
  382.9 3.4 copy-start.3
  399.9 181.0 %collective-permute-start.2 = (f32[64,64,512]{2,1,0:T(8,128)S(1)}, f32[64,64,512]{2,1,0:T(8,128)S(1)}, u32[]{:S(2)}, u32[]{:S(2)}) collective-permute-start(f32[64,64,512]{2,1,0:T(8,128)S(1)} %fusion.24), channel_id=1, source_target_pairs={{0,16},{8,24},{16,0},{24,8},{32,48},{40,56},{48,32},{56,40},{64,80... | collective-permute-start | bytes 25165832 | tf_op jit(solution)/shard_map/ppermute | solution.py:10
  580.9 3.4 copy-start.2
  598.3 119.9 %all-to-all-start = ((f32[8,1,8,64,512]{4,3,2,1,0:T(8,128)}), f32[8,1,8,64,512]{4,3,2,1,0:T(8,128)}, u32[]{:S(2)}, u32[]{:S(2)}) async-start(f32[8,1,8,64,512]{4,3,2,1,0:T(8,128)} %bitcast.40), calls=%async_computation | async-start | bytes 16777216 | tf_op jit(solution)/shard_map/all_to_all | solution.py:39
where the time goes:
time: 792 us; the launch traced here: 791 us
  waiting for transfers between devices  641 us (81%)
  matrix products  88.7 us (11%)
  local copies, waits for them, and re-layouts  47.3 us (6%)
  starting transfers between devices  13.9 us (2%)
    ppermute x3, waiting for transfers between devices, swapped(): return lax.ppermute(value, axis, pairs)  534 us
    all_to_all x1, waiting for transfers between devices, per_device(): lax.all_to_all(state.reshape(groups, 1, tail, rank, width), 'col', split_...  107 us
    dot_general x6, matrix products, mix_level(): jnp.einsum('...xy,...ys->...xs', weights, joined, precision=lax.Precision...  88.7 us
    rev x3, local copies, waits for them, and re-layouts, flip_axis(): return jnp.flip(values.reshape(split), axis=axis + 1).reshape(shape)  25.6 us
  transfers between devices with their start and end apart: 4, of which 4 were waited for; matrix products, arithmetic and copies ran while one was open for 1% of the time, Pallas kernels for 0%

commit v1 on v0

v1 whole, which is shorter than its diff:
```python
import jax
import jax.numpy as jnp
from jax import lax
from jax.experimental import pallas as pl
from jax.experimental.pallas import tpu as pltpu
from jax.sharding import PartitionSpec as P

MESH = pl.DeviceIdType.MESH
GROUP = 8
TAIL = 8
R = 64
S = 512
HALF = 256
LEVELS = 3


def split(value):
    high = value.astype(jnp.bfloat16)
    low = (value - high.astype(jnp.float32)).astype(jnp.bfloat16)
    return high, low


def dot(left, right):
    return jnp.dot(left, right, preferred_element_type=jnp.float32)


def mix_pair(weights, state, a, b):
    top = weights[a]
    bottom = pltpu.roll(weights[b], R, 1)
    wh, wl = split(jnp.concatenate([top, bottom], axis=0))
    for n in range(0, S, HALF):
        cols = pl.ds(n, HALF)
        xh, xl = split(jnp.concatenate([state[a, :, cols], state[b, :, cols]], axis=0))
        y = dot(wh, xh) + dot(wh, xl) + dot(wl, xh)
        state[a, :, cols] = y[:R]
        state[b, :, cols] = y[R:]


def mix_levels(weights, state):
    for level in range(LEVELS):
        stride = GROUP >> level + 1
        for a in range(GROUP):
            if not a & stride:
                mix_pair(weights.at[level], state, a, a | stride)


def kernel(x_ref, rw_ref, cw_ref, out_ref, xb, wb, zb, cb, xsem, wsem, zsem, csem, osem, ssem, vsem):
    row, col = lax.axis_index("row"), lax.axis_index("col")
    me, core = row // 2, row % 2

    barrier = pltpu.get_barrier_semaphore()

    def greet(step, carry):
        there = (2 * ((me + step // GROUP) % GROUP) + core, (col + step) % GROUP)
        pl.semaphore_signal(barrier, 1, device_id=there, device_id_type=MESH)
        return carry

    lax.fori_loop(1, GROUP * GROUP, greet, 0)
    pl.semaphore_wait(barrier, GROUP * GROUP - 1)

    def send_first(t, carry):
        for step in range(GROUP):
            a = (me + step) % GROUP
            block = ((a + col + t) % GROUP) * TAIL + t
            if step == 0:
                pltpu.make_async_copy(x_ref.at[block], xb.at[t, me], xsem.at[t]).start()
                pltpu.make_async_copy(rw_ref.at[:, block], wb.at[t, :, me], wsem.at[t]).start()
            else:
                there = (2 * a + core, col)
                pltpu.make_async_remote_copy(
                    x_ref.at[block], xb.at[t, me], ssem.at[0], xsem.at[t], device_id=there, device_id_type=MESH
                ).start()
                pltpu.make_async_remote_copy(
                    rw_ref.at[:, block], wb.at[t, :, me], ssem.at[1], wsem.at[t], device_id=there, device_id_type=MESH
                ).start()
        for j in range(GROUP):
            pltpu.make_async_copy(cw_ref.at[:, j * TAIL + t], cb.at[t, :, j], csem.at[t]).start()
        return carry

    lax.fori_loop(0, TAIL, send_first, 0)

    def whole(ref, sem):
        pltpu.make_async_copy(ref, ref, sem).wait()

    def row_step(t, carry):
        whole(xb.at[t], xsem.at[t])
        whole(wb.at[t], wsem.at[t])
        mix_levels(wb.at[t], xb.at[t])
        m = (me + col + t) % GROUP
        home = m == col
        for step in range(GROUP):
            i = (me + step) % GROUP

            def away():
                pltpu.make_async_remote_copy(
                    xb.at[t, i], zb.at[t, col], vsem, zsem.at[t], device_id=(2 * i + core, m), device_id_type=MESH
                ).start()

            if step == 0:
                @pl.when(home)
                def _():
                    pltpu.make_async_copy(xb.at[t, i], zb.at[t, col], zsem.at[t]).start()

                pl.when(jnp.logical_not(home))(away)
            else:
                away()
        return carry

    lax.fori_loop(0, TAIL, row_step, 0)

    def col_step(t, carry):
        whole(zb.at[t], zsem.at[t])
        whole(cb.at[t], csem.at[t])
        mix_levels(cb.at[t], zb.at[t])
        for j in range(GROUP):
            pltpu.make_async_copy(zb.at[t, j], out_ref.at[j * TAIL + t], osem).start()
        return carry

    lax.fori_loop(0, TAIL, col_step, 0)

    whole(zb, osem)
    whole(xb.at[pl.ds(0, TAIL), pl.ds(0, GROUP - 1)], ssem.at[0])
    whole(wb.at[pl.ds(0, TAIL), :, pl.ds(0, GROUP - 1)], ssem.at[1])
    whole(xb.at[pl.ds(0, TAIL), pl.ds(0, GROUP - 1)], vsem)
    whole(xb.at[0, pl.ds(0, TAIL - 1)], vsem)


def per_device(coeffs, row_weights, col_weights):
    blocks = GROUP * TAIL
    out = pl.pallas_call(
        kernel,
        out_shape=jax.ShapeDtypeStruct((blocks, R, S), jnp.float32),
        in_specs=[pl.BlockSpec(memory_space=pl.ANY)] * 3,
        out_specs=pl.BlockSpec(memory_space=pl.ANY),
        scratch_shapes=[
            pltpu.VMEM((TAIL, GROUP, R, S), jnp.float32),
            pltpu.VMEM((TAIL, LEVELS, GROUP, R, 2 * R), jnp.float32),
            pltpu.VMEM((TAIL, GROUP, R, S), jnp.float32),
            pltpu.VMEM((TAIL, LEVELS, GROUP, R, 2 * R), jnp.float32),
            pltpu.SemaphoreType.DMA((TAIL,)),
            pltpu.SemaphoreType.DMA((TAIL,)),
            pltpu.SemaphoreType.DMA((TAIL,)),
            pltpu.SemaphoreType.DMA((TAIL,)),
            pltpu.SemaphoreType.DMA,
            pltpu.SemaphoreType.DMA((2,)),
            pltpu.SemaphoreType.DMA,
        ],
        compiler_params=pltpu.CompilerParams(
            collective_id=0, has_side_effects=True, vmem_limit_bytes=48 * 1024 * 1024
        ),
        name="butterfly",
    )(
        coeffs.reshape(blocks, R, S),
        row_weights.reshape(LEVELS, blocks, R, 2 * R),
        col_weights.reshape(LEVELS, blocks, R, 2 * R),
    )
    return out.reshape(coeffs.shape)


def solution(mesh):
    return jax.shard_map(
        per_device,
        mesh=mesh,
        in_specs=(
            P("row", "col", None, None, None, None),
            P(None, "row", "col", None, None, None, None),
            P(None, "row", "col", None, None, None, None),
        ),
        out_specs=P("row", "col", None, None, None, None),
        check_vma=False,
    )
```

time: 792 us -> 313 us (0.40)
  the two profiles are of different devices: /device:TPU:0 before, /device:TPU:98 now
where the time goes in v1:
time: 313 us
  Pallas kernels  305 us (97%)
  local copies, waits for them, and re-layouts  8.58 us (3%)
    pallas_call x1, Pallas kernels, per_device(): pl.pallas_call(kernel, out_shape=jax.ShapeDtypeStruct((blocks, R, S), jnp...  305 us
    unnamed x1, local copies, waits for them, and re-layouts  8.58 us

profile of v1, /device:TPU:98, one launch (start us, length us, event | category | flops | bytes accessed | tf_op | source)
XLA Modules:
  0.0 313.3 jit_solution(16288804244899068136)
XLA Ops:
  0.0 304.7 %butterfly.1 = f32[64,64,512]{2,1,0:T(8,128)} custom-call(f32[64,64,512]{2,1,0:T(8,128)} %bitcast.5, f32[3,64,64,128]{3,2,1,0:T(8,128)} %bitcast.6, f32[3,64,64,128]{3,2,1,0:T(8,128)} %bitcast.7), custom_call_target="tpu_custom_call" | custom-call | tf_op jit(solution)/shard_map/butterfly/pallas_call | solution.py:130
  304.7 8.6 %copy.5 = f32[1,1,8,8,64,512]{5,4,3,2,1,0:T(8,128)} copy(f32[1,1,8,8,64,512]{5,4,3,2,1,0:T(8,128)} %bitcast.4) | data formatting | bytes 16777216

commit v2 on v0

v2 whole, which is shorter than its diff:
```python
import functools

import jax
import jax.numpy as jnp
from jax import lax
from jax.experimental import pallas as pl
from jax.experimental.pallas import tpu as pltpu
from jax.sharding import PartitionSpec as P

MESH = pl.DeviceIdType.MESH
RING = 4
PAIR = 2
GROUP = 8
TAIL = 8
R = 64
S = 512
HALF = 256
LEVELS = 3


def split(value):
    high = value.astype(jnp.bfloat16)
    low = (value - high.astype(jnp.float32)).astype(jnp.bfloat16)
    return high, low


def dot(left, right):
    return jnp.dot(left, right, preferred_element_type=jnp.float32)


def product(weights, value):
    wh, wl = weights
    xh, xl = split(value)
    return dot(wh, xh) + dot(wh, xl) + dot(wl, xh)


def mix_pair(first, second, state, a, b):
    weights = split(jnp.concatenate([first, pltpu.roll(second, R, 1)], axis=0))
    for n in range(0, S, HALF):
        cols = pl.ds(n, HALF)
        y = product(weights, jnp.concatenate([state[a, :, cols], state[b, :, cols]], axis=0))
        state[a, :, cols] = y[:R]
        state[b, :, cols] = y[R:]


def mix_level(weights, state, stride):
    for a in range(state.shape[0]):
        if not a & stride:
            b = a | stride
            mix_pair(weights(a), weights(b), state, a, b)


def mix_own(weights, state, partner, a):
    weights = split(weights)
    for n in range(0, S, HALF):
        cols = pl.ds(n, HALF)
        state[a, :, cols] = product(weights, jnp.concatenate([state[a, :, cols], partner[a, :, cols]], axis=0))


def kernel(
    x_ref, rw_ref, cw_ref, out_ref,
    xs, xp, xd, w0, wd, q, wb, x3, z4, zb, cb,
    xs_in, xp_in, xd_in, xo_in, w0_in, wd_in, wo_in, q_in, wb_in, x3_in, z4_in, zb_in, cb_in,
    sent, out_sem,
):
    row, column = lax.axis_index("row"), lax.axis_index("col")
    zl, y, core = row // GROUP, row // 2 % RING, row % 2
    x, zh = column // PAIR, column % PAIR
    near = 1 - zl
    far = 1 - zh

    def device(x, y, zh, zl):
        return (zl * GROUP + y * 2 + core, x * PAIR + zh)

    def remote(src, dst, kind, sem, there):
        pltpu.make_async_remote_copy(src, dst, sent.at[kind], sem, device_id=there, device_id_type=MESH).start()

    def local(src, dst, sem):
        pltpu.make_async_copy(src, dst, sem).start()

    def whole(ref, sem):
        pltpu.make_async_copy(ref, ref, sem).wait()

    barrier = pltpu.get_barrier_semaphore()
    partners = [device(x, y, zh, near)]
    for s in range(1, RING):
        partners += [device(x, (y + s) % RING, zh, zl), device((x + s) % RING, y, zh, zl)]
    partners += [device(x, y, far, side) for side in range(PAIR)]
    for there in partners:
        pl.semaphore_signal(barrier, 1, device_id=there, device_id_type=MESH)
    pl.semaphore_wait(barrier, len(partners))

    def send0(t):
        there = device(x, y, zh, near)
        remote(x_ref.at[:, zh, t], xp.at[t], 0, xp_in.at[t], there)
        local(x_ref.at[:, zh, t], xs.at[t], xs_in.at[t])
        local(rw_ref.at[0, :, zh, t], w0.at[t], w0_in.at[t])

    def send1(t):
        there = device(x, y, zh, near)
        for n in range(PAIR):
            mine = (x + PAIR * zl + n + t) % RING
            theirs = (x + PAIR * near + n + t) % RING
            remote(x_ref.at[theirs, far, t], xd.at[t, PAIR + n], 0, xd_in.at[t], there)
            remote(rw_ref.at[:, theirs, far, t], wd.at[t, PAIR + n], 1, wd_in.at[t], there)
            local(x_ref.at[mine, far, t], xd.at[t, n], xo_in.at[t])
            local(rw_ref.at[:, mine, far, t], wd.at[t, n], wo_in.at[t])

    def factor(t):
        local(cw_ref.at[:, :, t], cb.at[t], cb_in.at[t])
        for s in range(RING):
            yd = (y + s) % RING
            src, dst = rw_ref.at[pl.ds(1, 2), (x + yd + t) % RING, zh, t], wb.at[t, 0, y]
            if s == 0:
                local(src, dst, wb_in.at[t, 0])
            else:
                remote(src, dst, 2, wb_in.at[t, 0], device(x, yd, zh, zl))

    def across(t, side):
        return (zl + y // 2 + t + side) % 2

    def pair0(t):
        whole(xs.at[t], xs_in.at[t])
        whole(w0.at[t], w0_in.at[t])
        whole(xp.at[t], xp_in.at[t])
        for a in range(RING):
            mix_own(w0[t, a], xs.at[t], xp.at[t], a)
        for s in range(RING):
            yd = (y + s) % RING
            src, dst = xs.at[t, (x + yd + t) % RING], q.at[t, 0, y]
            if s == 0:
                local(src, dst, q_in.at[t, 0])
            else:
                remote(src, dst, 3, q_in.at[t, 0], device(x, yd, zh, zl))

    def pair1(t):
        whole(xd.at[t, pl.ds(0, PAIR)], xo_in.at[t])
        whole(xd.at[t, pl.ds(PAIR, PAIR)], xd_in.at[t])
        whole(wd.at[t, pl.ds(0, PAIR)], wo_in.at[t])
        whole(wd.at[t, pl.ds(PAIR, PAIR)], wd_in.at[t])
        for a in range(PAIR):
            mix_pair(wd[t, a, 0], wd[t, PAIR + a, 0], xd.at[t], a, PAIR + a)
        for s in range(RING):
            yd = (y + s) % RING
            there = device(x, yd, zh, zl)
            e = (yd + PAIR * (t + zh)) % RING
            src, dst = xd.at[t, e], q.at[t, 1, y]
            wsrc, wdst = wd.at[t, e, pl.ds(1, 2)], wb.at[t, 1, y]
            if s == 0:
                local(src, dst, q_in.at[t, 1])
                local(wsrc, wdst, wb_in.at[t, 1])
            else:
                remote(wsrc, wdst, 2, wb_in.at[t, 1], there)
                remote(src, dst, 3, q_in.at[t, 1], there)

    def ring_step(t, part):
        whole(wb.at[t, part], wb_in.at[t, part])
        whole(q.at[t, part], q_in.at[t, part])
        for level in range(2):
            mix_level(lambda a: wb[t, part, a, level], q.at[t, part], 2 >> level)
        shift = (y if part == 0 else PAIR * zl + y % 2) + t
        src, dst, sem = q.at[t, part], x3.at[t, part], x3_in.at[t, part]
        at_home = shift % RING == 0
        pl.when(at_home)(lambda: local(src, dst, sem))
        pl.when(jnp.logical_not(at_home))(
            lambda: remote(src, dst, 4, sem, device((x + shift) % RING, y, zh, zl))
        )

    def ring0(t):
        ring_step(t, 0)

    def ring1(t):
        ring_step(t, 1)

    def give_back(held, t, j):
        for s in range(RING):
            yi = (y + s) % RING
            src, dst = held.at[yi], zb.at[t, j]
            if s == 0:
                local(src, dst, zb_in.at[t])
            else:
                remote(src, dst, 6, zb_in.at[t], device(x, yi, zh, zl))

    def turn1(t):
        whole(x3.at[t, 1], x3_in.at[t, 1])
        remote(x3.at[t, 1], z4.at[t], 5, z4_in.at[t], device(x, y, far, across(t, zh)))

    def back0(t):
        whole(x3.at[t, 0], x3_in.at[t, 0])
        give_back(x3.at[t, 0], t, PAIR * ((x - y - t + 16) % RING) + zh)

    def back1(t):
        whole(z4.at[t], z4_in.at[t])
        give_back(z4.at[t], t, PAIR * ((x - PAIR * across(t, far) - y % 2 - t + 16) % RING) + far)

    def col(t):
        whole(cb.at[t], cb_in.at[t])
        whole(zb.at[t], zb_in.at[t])
        for level in range(LEVELS):
            mix_level(lambda a: cb[t, level, a], zb.at[t], GROUP >> level + 1)
        local(zb.at[t], out_ref.at[:, t], out_sem)

    order = (
        (send1, 2),
        (send0, 3),
        (factor, 0),
        (pair1, 3),
        (ring1, 4),
        (pair0, 4),
        (turn1, 5),
        (ring0, 5),
        (back1, 6),
        (back0, 6),
        (col, 7),
    )
    last = max(lag for _, lag in order)

    def step(n, carry):
        for work, lag in order:
            pl.when((n >= lag) & (n < TAIL + lag))(functools.partial(work, n - lag))
        return carry

    lax.fori_loop(0, TAIL + last, step, 0)

    whole(zb, out_sem)
    whole(xp, sent.at[0])
    whole(xd.at[:, pl.ds(0, PAIR)], sent.at[0])
    whole(wd.at[:, pl.ds(0, PAIR)], sent.at[1])
    whole(wb.at[:, :, pl.ds(0, RING - 1)], sent.at[2])
    whole(q.at[:, :, pl.ds(0, RING - 1)], sent.at[3])
    whole(x3.at[pl.ds(0, TAIL - TAIL // RING)], sent.at[4])
    whole(z4, sent.at[5])
    whole(zb.at[:, pl.ds(0, GROUP - PAIR)], sent.at[6])


def per_device(coeffs, row_weights, col_weights):
    block, factor = (R, S), (R, 2 * R)
    buffers = [
        (TAIL, RING) + block,
        (TAIL, RING) + block,
        (TAIL, RING) + block,
        (TAIL, RING) + factor,
        (TAIL, RING, LEVELS) + factor,
        (TAIL, PAIR, RING) + block,
        (TAIL, PAIR, RING, LEVELS - 1) + factor,
        (TAIL, PAIR, RING) + block,
        (TAIL, RING) + block,
        (TAIL, GROUP) + block,
        (TAIL, LEVELS, GROUP) + factor,
    ]
    out = pl.pallas_call(
        kernel,
        out_shape=jax.ShapeDtypeStruct((GROUP, TAIL) + block, jnp.float32),
        in_specs=[pl.BlockSpec(memory_space=pl.ANY)] * 3,
        out_specs=pl.BlockSpec(memory_space=pl.ANY),
        scratch_shapes=[pltpu.VMEM(shape, jnp.float32) for shape in buffers]
        + [pltpu.SemaphoreType.DMA((TAIL,))] * 7
        + [pltpu.SemaphoreType.DMA((TAIL, PAIR))] * 3
        + [pltpu.SemaphoreType.DMA((TAIL,))] * 3
        + [pltpu.SemaphoreType.DMA((7,)), pltpu.SemaphoreType.DMA],
        compiler_params=pltpu.CompilerParams(
            collective_id=0, has_side_effects=True, vmem_limit_bytes=60 * 1024 * 1024
        ),
        name="butterfly",
    )(
        coeffs.reshape((RING, PAIR, TAIL) + block),
        row_weights.reshape((LEVELS, RING, PAIR, TAIL) + factor),
        col_weights.reshape((LEVELS, GROUP, TAIL) + factor),
    )
    return out.reshape(coeffs.shape)


def solution(mesh):
    return jax.shard_map(
        per_device,
        mesh=mesh,
        in_specs=(
            P("row", "col", None, None, None, None),
            P(None, "row", "col", None, None, None, None),
            P(None, "row", "col", None, None, None, None),
        ),
        out_specs=P("row", "col", None, None, None, None),
        check_vma=False,
    )
```

time: 792 us -> 270 us (0.34)
  waiting for transfers between devices: 641 us -> 0 us
  Pallas kernels: 0 us -> 261 us
  matrix products: 88.7 us -> 0 us
  local copies, waits for them, and re-layouts: 47.3 us -> 8.58 us
  starting transfers between devices: 13.9 us -> 0 us
    ppermute x3 -> x0, waiting for transfers between devices: 534 us -> none  [swapped(): return lax.ppermute(value, axis, pairs)]
    pallas_call x0 -> x1, Pallas kernels: none -> 261 us  [per_device(): pl.pallas_call(kernel, out_shape=jax.ShapeDtypeStruct((GROUP, TAIL) + blo...]
    all_to_all x1 -> x0, waiting for transfers between devices: 107 us -> none  [per_device(): lax.all_to_all(state.reshape(groups, 1, tail, rank, width), 'col', split_...]
    dot_general x6 -> x0, matrix products: 88.7 us -> none  [mix_level(): jnp.einsum('...xy,...ys->...xs', weights, joined, precision=lax.Precision...]
    rev x3 -> x0, local copies, waits for them, and re-layouts: 25.6 us -> none  [flip_axis(): return jnp.flip(values.reshape(split), axis=axis + 1).reshape(shape)]
    slice x2 -> x0, local copies, waits for them, and re-layouts: 11.5 us -> none  [the longest x1 5.76 us: per_device(): weights = col_weights[level].reshape(blocks, rank, 2 * rank)]
  transfers between devices with their start and end apart: 4 -> 0, of which waited for: 4 -> 0; matrix products, arithmetic and copies ran while one was open for 1% -> 0% of each run, Pallas kernels for 0% -> 0%
where the time goes in v2:
time: 270 us
  Pallas kernels  261 us (97%)
  local copies, waits for them, and re-layouts  8.58 us (3%)
    pallas_call x1, Pallas kernels, per_device(): pl.pallas_call(kernel, out_shape=jax.ShapeDtypeStruct((GROUP, TAIL) + blo...  261 us
    unnamed x1, local copies, waits for them, and re-layouts  8.58 us

profile of v2, /device:TPU:0, one launch (start us, length us, event | category | flops | bytes accessed | tf_op | source)
XLA Modules:
  0.0 269.8 jit_solution(10829093100542837367)
XLA Ops:
  0.0 261.2 %butterfly.1 = f32[8,8,64,512]{3,2,1,0:T(8,128)} custom-call(f32[4,2,8,64,512]{4,3,2,1,0:T(8,128)} %bitcast.5, f32[3,4,2,8,64,128]{5,4,3,2,1,0:T(8,128)} %bitcast.6, f32[3,8,8,64,128]{4,3,2,1,0:T(8,128)} %bitcast.7), custom_call_target="tpu_custom_call" | custom-call | tf_op jit(solution)/shard_map/butterfly/pallas_call | solution.py:251
  261.3 8.6 %copy.5 = f32[1,1,8,8,64,512]{5,4,3,2,1,0:T(8,128)} copy(f32[1,1,8,8,64,512]{5,4,3,2,1,0:T(8,128)} %bitcast.4) | data formatting | bytes 16777216

commit v3 on v2

v3 whole, which is shorter than its diff:
```python
import functools

import jax
import jax.numpy as jnp
from jax import lax
from jax.experimental import pallas as pl
from jax.experimental.pallas import tpu as pltpu
from jax.sharding import PartitionSpec as P

MESH = pl.DeviceIdType.MESH
RING = 4
PAIR = 2
GROUP = 8
TAIL = 8
R = 64
S = 512
PIECES = 2
WIDTH = S // PIECES
STEPS = TAIL * PIECES
LEVELS = 3


def split(value):
    high = value.astype(jnp.bfloat16)
    low = (value - high.astype(jnp.float32)).astype(jnp.bfloat16)
    return high, low


def dot(left, right):
    return jnp.dot(left, right, preferred_element_type=jnp.float32)


def product(weights, value):
    wh, wl = weights
    xh, xl = split(value)
    return dot(wh, xh) + dot(wh, xl) + dot(wl, xh)


def mix_pair(first, second, state, a, b):
    weights = split(jnp.concatenate([first, pltpu.roll(second, R, 1)], axis=0))
    y = product(weights, jnp.concatenate([state[a], state[b]], axis=0))
    state[a] = y[:R]
    state[b] = y[R:]


def mix_level(weights, state, stride):
    for a in range(state.shape[0]):
        if not a & stride:
            b = a | stride
            mix_pair(weights(a), weights(b), state, a, b)


def mix_own(weights, state, partner, a):
    state[a] = product(split(weights), jnp.concatenate([state[a], partner[a]], axis=0))


def kernel(
    x_ref, rw_ref, cw_ref, zb,
    xs, xp, xd, w0, wd, q, wb, x3, z4, cb,
    xs_in, xp_in, xd_in, xo_in, w0_in, wd_in, wo_in, q_in, wb_in, x3_in, z4_in, zb_in, cb_in,
    sent,
):
    row, column = lax.axis_index("row"), lax.axis_index("col")
    zl, y, core = row // GROUP, row // 2 % RING, row % 2
    x, zh = column // PAIR, column % PAIR
    near = 1 - zl
    far = 1 - zh

    def device(x, y, zh, zl):
        return (zl * GROUP + y * 2 + core, x * PAIR + zh)

    def remote(src, dst, kind, sem, there):
        pltpu.make_async_remote_copy(src, dst, sent.at[kind], sem, device_id=there, device_id_type=MESH).start()

    def local(src, dst, sem):
        pltpu.make_async_copy(src, dst, sem).start()

    def whole(ref, sem):
        pltpu.make_async_copy(ref, ref, sem).wait()

    barrier = pltpu.get_barrier_semaphore()
    partners = [device(x, y, zh, near)]
    for s in range(1, RING):
        partners += [device(x, (y + s) % RING, zh, zl), device((x + s) % RING, y, zh, zl)]
    partners += [device(x, y, far, side) for side in range(PAIR)]
    for there in partners:
        pl.semaphore_signal(barrier, 1, device_id=there, device_id_type=MESH)
    pl.semaphore_wait(barrier, len(partners))

    def piece(n):
        return n // PIECES, pl.ds(pl.multiple_of(n % PIECES * WIDTH, WIDTH), WIDTH)

    def once(n, work):
        pl.when(n % PIECES == 0)(work)

    def send0(n):
        t, cols = piece(n)
        remote(x_ref.at[:, zh, t, :, cols], xp.at[n], 0, xp_in.at[n], device(x, y, zh, near))
        local(x_ref.at[:, zh, t, :, cols], xs.at[n], xs_in.at[n])
        once(n, lambda: local(rw_ref.at[0, :, zh, t], w0.at[t], w0_in.at[t]))

    def send1(n):
        t, cols = piece(n)
        there = device(x, y, zh, near)
        for a in range(PAIR):
            mine = (x + PAIR * zl + a + t) % RING
            theirs = (x + PAIR * near + a + t) % RING

            @functools.partial(once, n)
            def _():
                remote(rw_ref.at[:, theirs, far, t], wd.at[t, PAIR + a], 1, wd_in.at[t], there)
                local(rw_ref.at[:, mine, far, t], wd.at[t, a], wo_in.at[t])

            remote(x_ref.at[theirs, far, t, :, cols], xd.at[n, PAIR + a], 0, xd_in.at[n], there)
            local(x_ref.at[mine, far, t, :, cols], xd.at[n, a], xo_in.at[n])

    def send_factor(src, dst, sem, s, yd):
        if s == 0:
            local(src, dst, sem)
        else:
            remote(src, dst, 2, sem, device(x, yd, zh, zl))

    def factor(n):
        t, _ = piece(n)

        @functools.partial(once, n)
        def _():
            local(cw_ref.at[:, :, t], cb.at[t], cb_in.at[t])
            for s in range(RING):
                yd = (y + s) % RING
                send_factor(rw_ref.at[pl.ds(1, 2), (x + yd + t) % RING, zh, t], wb.at[t, 0, y], wb_in.at[t, 0], s, yd)

    def across(t, side):
        return (zl + y // 2 + t + side) % 2

    def spread(src, dst, sem, s, yd):
        if s == 0:
            local(src, dst, sem)
        else:
            remote(src, dst, 3, sem, device(x, yd, zh, zl))

    def pair0(n):
        t, _ = piece(n)
        once(n, lambda: whole(w0.at[t], w0_in.at[t]))
        whole(xs.at[n], xs_in.at[n])
        whole(xp.at[n], xp_in.at[n])
        for a in range(RING):
            mix_own(w0[t, a], xs.at[n], xp.at[n], a)
        for s in range(RING):
            yd = (y + s) % RING
            spread(xs.at[n, (x + yd + t) % RING], q.at[n, 0, y], q_in.at[n, 0], s, yd)

    def pair1(n):
        t, _ = piece(n)

        @functools.partial(once, n)
        def _():
            whole(wd.at[t, pl.ds(0, PAIR)], wo_in.at[t])
            whole(wd.at[t, pl.ds(PAIR, PAIR)], wd_in.at[t])
            for s in range(RING):
                yd = (y + s) % RING
                e = (yd + PAIR * (t + zh)) % RING
                send_factor(wd.at[t, e, pl.ds(1, 2)], wb.at[t, 1, y], wb_in.at[t, 1], s, yd)

        whole(xd.at[n, pl.ds(0, PAIR)], xo_in.at[n])
        whole(xd.at[n, pl.ds(PAIR, PAIR)], xd_in.at[n])
        for a in range(PAIR):
            mix_pair(wd[t, a, 0], wd[t, PAIR + a, 0], xd.at[n], a, PAIR + a)
        for s in range(RING):
            yd = (y + s) % RING
            spread(xd.at[n, (yd + PAIR * (t + zh)) % RING], q.at[n, 1, y], q_in.at[n, 1], s, yd)

    def ring_step(n, part):
        t, _ = piece(n)
        once(n, lambda: whole(wb.at[t, part], wb_in.at[t, part]))
        whole(q.at[n, part], q_in.at[n, part])
        for level in range(2):
            mix_level(lambda a: wb[t, part, a, level], q.at[n, part], 2 >> level)
        shift = (y if part == 0 else PAIR * zl + y % 2) + t
        src, dst, sem = q.at[n, part], x3.at[n, part], x3_in.at[n, part]
        at_home = shift % RING == 0
        pl.when(at_home)(lambda: local(src, dst, sem))
        pl.when(jnp.logical_not(at_home))(
            lambda: remote(src, dst, 4, sem, device((x + shift) % RING, y, zh, zl))
        )

    def ring0(n):
        ring_step(n, 0)

    def ring1(n):
        ring_step(n, 1)

    def give_back(held, n, j):
        t, cols = piece(n)
        for s in range(RING):
            yi = (y + s) % RING
            src, dst = held.at[yi], zb.at[j, t, :, cols]
            if s == 0:
                local(src, dst, zb_in.at[n])
            else:
                remote(src, dst, 6, zb_in.at[n], device(x, yi, zh, zl))

    def turn1(n):
        t, _ = piece(n)
        whole(x3.at[n, 1], x3_in.at[n, 1])
        remote(x3.at[n, 1], z4.at[n], 5, z4_in.at[n], device(x, y, far, across(t, zh)))

    def back0(n):
        t, _ = piece(n)
        whole(x3.at[n, 0], x3_in.at[n, 0])
        give_back(x3.at[n, 0], n, PAIR * ((x - y - t + 16) % RING) + zh)

    def back1(n):
        t, _ = piece(n)
        whole(z4.at[n], z4_in.at[n])
        give_back(z4.at[n], n, PAIR * ((x - PAIR * across(t, far) - y % 2 - t + 16) % RING) + far)

    def col(n):
        t, cols = piece(n)
        once(n, lambda: whole(cb.at[t], cb_in.at[t]))
        state = zb.at[:, t, :, cols]
        whole(state, zb_in.at[n])
        for level in range(LEVELS):
            mix_level(lambda a: cb[t, level, a], state, GROUP >> level + 1)

    order = (
        (send1, 4),
        (factor, 0),
        (pair1, 5),
        (ring1, 6),
        (send0, 5),
        (turn1, 6),
        (pair0, 6),
        (ring0, 7),
        (back1, 7),
        (back0, 8),
        (col, 9),
    )
    last = max(lag for _, lag in order)

    def step(n, carry):
        for work, lag in order:
            pl.when((n >= lag) & (n < STEPS + lag))(functools.partial(work, n - lag))
        return carry

    lax.fori_loop(0, STEPS + last, step, 0)

    whole(xp, sent.at[0])
    whole(xd.at[:, pl.ds(0, PAIR)], sent.at[0])
    whole(wd.at[:, pl.ds(0, PAIR)], sent.at[1])
    whole(wb.at[:, :, pl.ds(0, RING - 1)], sent.at[2])
    whole(q.at[:, :, pl.ds(0, RING - 1)], sent.at[3])
    whole(x3.at[pl.ds(0, STEPS - STEPS // RING)], sent.at[4])
    whole(z4, sent.at[5])
    whole(zb.at[pl.ds(0, GROUP - PAIR)], sent.at[6])


def per_device(coeffs, row_weights, col_weights):
    block, factor, part = (R, S), (R, 2 * R), (R, WIDTH)
    buffers = [
        (STEPS, RING) + part,
        (STEPS, RING) + part,
        (STEPS, RING) + part,
        (TAIL, RING) + factor,
        (TAIL, RING, LEVELS) + factor,
        (STEPS, PAIR, RING) + part,
        (TAIL, PAIR, RING, LEVELS - 1) + factor,
        (STEPS, PAIR, RING) + part,
        (STEPS, RING) + part,
        (TAIL, LEVELS, GROUP) + factor,
    ]
    out = pl.pallas_call(
        kernel,
        out_shape=pltpu.VMEM((GROUP, TAIL) + block, jnp.float32),
        in_specs=[pl.BlockSpec(memory_space=pl.ANY)] * 3,
        out_specs=pl.BlockSpec(memory_space=pltpu.VMEM),
        scratch_shapes=[pltpu.VMEM(shape, jnp.float32) for shape in buffers]
        + [pltpu.SemaphoreType.DMA((STEPS,))] * 4
        + [pltpu.SemaphoreType.DMA((TAIL,))] * 3
        + [pltpu.SemaphoreType.DMA((STEPS, PAIR))]
        + [pltpu.SemaphoreType.DMA((TAIL, PAIR))]
        + [pltpu.SemaphoreType.DMA((STEPS, PAIR))]
        + [pltpu.SemaphoreType.DMA((STEPS,))] * 2
        + [pltpu.SemaphoreType.DMA((TAIL,))]
        + [pltpu.SemaphoreType.DMA((7,))],
        compiler_params=pltpu.CompilerParams(
            collective_id=0, has_side_effects=True, vmem_limit_bytes=50 * 1024 * 1024
        ),
        name="butterfly",
    )(
        coeffs.reshape((RING, PAIR, TAIL) + block),
        row_weights.reshape((LEVELS, RING, PAIR, TAIL) + factor),
        col_weights.reshape((LEVELS, GROUP, TAIL) + factor),
    )
    return out.reshape(coeffs.shape)


def solution(mesh):
    return jax.shard_map(
        per_device,
        mesh=mesh,
        in_specs=(
            P("row", "col", None, None, None, None),
            P(None, "row", "col", None, None, None, None),
            P(None, "row", "col", None, None, None, None),
        ),
        out_specs=P("row", "col", None, None, None, None),
        check_vma=False,
    )
```

time: 270 us -> 256 us (0.948)
  Pallas kernels: 261 us -> 252 us
  local copies, waits for them, and re-layouts: 8.58 us -> 3.4 us
    pallas_call x1, Pallas kernels: 261 us -> 252 us  [per_device(): pl.pallas_call(kernel, out_shape=pltpu.VMEM((GROUP, TAIL) + block, jnp.fl...]
    unnamed x1, local copies, waits for them, and re-layouts: 8.58 us -> 3.4 us
where the time goes in v3:
time: 256 us
  Pallas kernels  252 us (98%)
  local copies, waits for them, and re-layouts  3.4 us (1%)
    pallas_call x1, Pallas kernels, per_device(): pl.pallas_call(kernel, out_shape=pltpu.VMEM((GROUP, TAIL) + block, jnp.fl...  252 us

profile of v3, /device:TPU:0, one launch (start us, length us, event | category | flops | bytes accessed | tf_op | source)
XLA Modules:
  0.0 255.5 jit_solution(15962531553880067161)
XLA Ops:
  0.0 252.1 %butterfly.1 = f32[8,8,64,512]{3,2,1,0:T(8,128)S(1)} custom-call(f32[4,2,8,64,512]{4,3,2,1,0:T(8,128)} %bitcast.5, f32[3,4,2,8,64,128]{5,4,3,2,1,0:T(8,128)} %bitcast.6, f32[3,8,8,64,128]{4,3,2,1,0:T(8,128)} %bitcast.7), custom_call_target="tpu_custom_call" | custom-call | tf_op jit(solution)/shard_map/butterfly/pallas_call | solution.py:272
  252.1 3.4 %copy.5 = f32[1,1,8,8,64,512]{5,4,3,2,1,0:T(8,128)} copy(f32[1,1,8,8,64,512]{5,4,3,2,1,0:T(8,128)S(1)} %bitcast.4) | data formatting | bytes 16777216

commit v4 on v3

--- a/solution.py
+++ b/solution.py
@@ -224,17 +224,17 @@
             mix_level(lambda a: cb[t, level, a], state, GROUP >> level + 1)
 
     order = (
+        (col, 12),
         (send1, 4),
+        (turn1, 8),
         (factor, 0),
+        (back1, 10),
+        (back0, 9),
+        (ring0, 8),
+        (ring1, 6),
         (pair1, 5),
-        (ring1, 6),
-        (send0, 5),
-        (turn1, 6),
-        (pair0, 6),
-        (ring0, 7),
-        (back1, 7),
-        (back0, 8),
-        (col, 9),
+        (pair0, 7),
+        (send0, 6),
     )
     last = max(lag for _, lag in order)
 

time: 256 us -> 251 us (0.980)
  Pallas kernels: 252 us -> 245 us
    pallas_call x1, Pallas kernels: 252 us -> 245 us  [per_device(): pl.pallas_call(kernel, out_shape=pltpu.VMEM((GROUP, TAIL) + block, jnp.fl...]
where the time goes in v4:
time: 251 us; the launch traced here: 248 us
  Pallas kernels  245 us (98%)
  local copies, waits for them, and re-layouts  3.4 us (1%)
    pallas_call x1, Pallas kernels, per_device(): pl.pallas_call(kernel, out_shape=pltpu.VMEM((GROUP, TAIL) + block, jnp.fl...  245 us

profile of v4, /device:TPU:0, one launch (start us, length us, event | category | flops | bytes accessed | tf_op | source)
XLA Modules:
  0.0 248.1 jit_solution(17843853805390806244)
XLA Ops:
  0.0 244.7 %butterfly.1 = f32[8,8,64,512]{3,2,1,0:T(8,128)S(1)} custom-call(f32[4,2,8,64,512]{4,3,2,1,0:T(8,128)} %bitcast.5, f32[3,4,2,8,64,128]{5,4,3,2,1,0:T(8,128)} %bitcast.6, f32[3,8,8,64,128]{4,3,2,1,0:T(8,128)} %bitcast.7), custom_call_target="tpu_custom_call" | custom-call | tf_op jit(solution)/shard_map/butterfly/pallas_call | solution.py:272
  244.7 3.4 %copy.5 = f32[1,1,8,8,64,512]{5,4,3,2,1,0:T(8,128)} copy(f32[1,1,8,8,64,512]{5,4,3,2,1,0:T(8,128)S(1)} %bitcast.4) | data formatting | bytes 16777216

commit v5 on v4

--- a/solution.py
+++ b/solution.py
@@ -26,14 +26,14 @@
     return high, low
 
 
-def dot(left, right):
-    return jnp.dot(left, right, preferred_element_type=jnp.float32)
-
-
 def product(weights, value):
     wh, wl = weights
     xh, xl = split(value)
-    return dot(wh, xh) + dot(wh, xl) + dot(wl, xh)
+    return jnp.dot(
+        jnp.concatenate([wh, wl, wh], axis=1),
+        jnp.concatenate([xh, xh, xl], axis=0),
+        preferred_element_type=jnp.float32,
+    )
 
 
 def mix_pair(first, second, state, a, b):
@@ -87,11 +87,15 @@
         pl.semaphore_signal(barrier, 1, device_id=there, device_id_type=MESH)
     pl.semaphore_wait(barrier, len(partners))
 
+    def place(n):
+        return n // PIECES, n % PIECES
+
     def piece(n):
-        return n // PIECES, pl.ds(pl.multiple_of(n % PIECES * WIDTH, WIDTH), WIDTH)
+        t, part = place(n)
+        return t, pl.ds(pl.multiple_of(part * WIDTH, WIDTH), WIDTH)
 
     def once(n, work):
-        pl.when(n % PIECES == 0)(work)
+        pl.when(place(n)[1] == 0)(work)
 
     def send0(n):
         t, cols = piece(n)
@@ -226,15 +230,15 @@
     order = (
         (col, 12),
         (send1, 4),
+        (back1, 10),
         (turn1, 8),
         (factor, 0),
-        (back1, 10),
         (back0, 9),
         (ring0, 8),
         (ring1, 6),
         (pair1, 5),
+        (send0, 6),
         (pair0, 7),
-        (send0, 6),
     )
     last = max(lag for _, lag in order)
 

time: 251 us -> 247 us (0.984); the launches traced: 248 us -> 247 us
  no operation moved by 1% of the time
where the time goes in v5:
time: 247 us
  Pallas kernels  243 us (98%)
  local copies, waits for them, and re-layouts  3.4 us (1%)
    pallas_call x1, Pallas kernels, per_device(): pl.pallas_call(kernel, out_shape=pltpu.VMEM((GROUP, TAIL) + block, jnp.fl...  243 us

profile of v5, /device:TPU:0, one launch (start us, length us, event | category | flops | bytes accessed | tf_op | source)
XLA Modules:
  0.0 246.9 jit_solution(13092183821049543455)
XLA Ops:
  0.0 243.4 %butterfly.1 = f32[8,8,64,512]{3,2,1,0:T(8,128)S(1)} custom-call(f32[4,2,8,64,512]{4,3,2,1,0:T(8,128)} %bitcast.5, f32[3,4,2,8,64,128]{5,4,3,2,1,0:T(8,128)} %bitcast.6, f32[3,8,8,64,128]{4,3,2,1,0:T(8,128)} %bitcast.7), custom_call_target="tpu_custom_call" | custom-call | tf_op jit(solution)/shard_map/butterfly/pallas_call | solution.py:276
  243.5 3.4 %copy.5 = f32[1,1,8,8,64,512]{5,4,3,2,1,0:T(8,128)} copy(f32[1,1,8,8,64,512]{5,4,3,2,1,0:T(8,128)S(1)} %bitcast.4) | data formatting | bytes 16777216

commit v6 on v5

--- a/solution.py
+++ b/solution.py
@@ -14,7 +14,7 @@
 TAIL = 8
 R = 64
 S = 512
-PIECES = 2
+PIECES = 4
 WIDTH = S // PIECES
 STEPS = TAIL * PIECES
 LEVELS = 3
@@ -228,17 +228,17 @@
             mix_level(lambda a: cb[t, level, a], state, GROUP >> level + 1)
 
     order = (
-        (col, 12),
-        (send1, 4),
-        (back1, 10),
-        (turn1, 8),
+        (col, 25),
+        (send1, 8),
+        (back1, 20),
+        (turn1, 16),
         (factor, 0),
-        (back0, 9),
-        (ring0, 8),
-        (ring1, 6),
-        (pair1, 5),
-        (send0, 6),
-        (pair0, 7),
+        (back0, 19),
+        (ring0, 17),
+        (ring1, 13),
+        (pair1, 11),
+        (send0, 12),
+        (pair0, 15),
     )
     last = max(lag for _, lag in order)
 

time: 247 us -> 244 us (0.988)
  Pallas kernels: 243 us -> 240 us
    pallas_call x1, Pallas kernels: 243 us -> 240 us  [per_device(): pl.pallas_call(kernel, out_shape=pltpu.VMEM((GROUP, TAIL) + block, jnp.fl...]
where the time goes in v6:
time: 244 us; the launch traced here: 243 us
  Pallas kernels  240 us (98%)
  local copies, waits for them, and re-layouts  3.4 us (1%)
    pallas_call x1, Pallas kernels, per_device(): pl.pallas_call(kernel, out_shape=pltpu.VMEM((GROUP, TAIL) + block, jnp.fl...  240 us

profile of v6, /device:TPU:0, one launch (start us, length us, event | category | flops | bytes accessed | tf_op | source)
XLA Modules:
  0.0 242.9 jit_solution(3730136169251079886)
XLA Ops:
  0.0 239.5 %butterfly.1 = f32[8,8,64,512]{3,2,1,0:T(8,128)S(1)} custom-call(f32[4,2,8,64,512]{4,3,2,1,0:T(8,128)} %bitcast.5, f32[3,4,2,8,64,128]{5,4,3,2,1,0:T(8,128)} %bitcast.6, f32[3,8,8,64,128]{4,3,2,1,0:T(8,128)} %bitcast.7), custom_call_target="tpu_custom_call" | custom-call | tf_op jit(solution)/shard_map/butterfly/pallas_call | solution.py:276
  239.5 3.4 %copy.5 = f32[1,1,8,8,64,512]{5,4,3,2,1,0:T(8,128)} copy(f32[1,1,8,8,64,512]{5,4,3,2,1,0:T(8,128)S(1)} %bitcast.4) | data formatting | bytes 16777216
